TPU v7x, 128 devices: a whole 4x4x4 slice. The times are simulated.
128 devices in a mesh: dp: 64 (over x, y, z), mp: 2 (over core).
Axes of the slice: x: 4, y: 4, z: 4, core: 2. Of those that a mesh axis runs over, the one named last changes fastest.
Arguments:
- hidden_in: bfloat16 [8192, 896], P('dp'), may hold values from -6 to 6
- cotangent: bfloat16 [3, 8192, 896], P(None, 'dp'), may hold values from -6 to 6
- lengths: int32 [64, 3], P('dp'), may hold values from 1 to 64, 128 in all within a row
- gains: float32 [4, 896], replicated, may hold values from 0.5 to 1.5
- query_codes: bfloat16 [896, 896], P('dp', 'mp'), may hold values from 0 to 255, as said below
- key_codes: bfloat16 [896, 128], P('dp', 'mp'), may hold values from 0 to 255, as said below
- value_codes: bfloat16 [896, 128], P('dp', 'mp'), may hold values from 0 to 255, as said below
- output_codes: bfloat16 [896, 896], P('mp', 'dp'), may hold values from 0 to 255, as said below
- gate_codes: bfloat16 [896, 4864], P('dp', 'mp'), may hold values from 0 to 255, as said below
- upward_codes: bfloat16 [896, 4864], P('dp', 'mp'), may hold values from 0 to 255, as said below
- down_codes: bfloat16 [4864, 896], P('mp', 'dp'), may hold values from 0 to 255, as said below
- query_scale: float32 [896], P('mp'), as said below
- key_scale: float32 [128], P('mp'), as said below
- value_scale: float32 [128], P('mp'), as said below
- output_scale: float32 [896], replicated, as said below
- gate_scale: float32 [4864], P('mp'), as said below
- upward_scale: float32 [4864], P('mp'), as said below
- down_scale: float32 [896], replicated, as said below
Outputs:
- result: bfloat16 [3, 8192, 896], P(None, 'dp')
- input_grad: bfloat16 [8192, 896], P('dp')
- query_grad: float32 [896, 896], P('dp', 'mp')
- key_grad: float32 [896, 128], P('dp', 'mp')
- value_grad: float32 [896, 128], P('dp', 'mp')
- output_grad: float32 [896, 896], P('mp', 'dp')
- gate_grad: float32 [896, 4864], P('dp', 'mp')
- upward_grad: float32 [896, 4864], P('dp', 'mp')
- down_grad: float32 [4864, 896], P('mp', 'dp')
- query_scale_grad: float32 [896], P('mp')
- key_scale_grad: float32 [128], P('mp')
- value_scale_grad: float32 [128], P('mp')
- output_scale_grad: float32 [896], replicated
- gate_scale_grad: float32 [4864], P('mp')
- upward_scale_grad: float32 [4864], P('mp')
- down_scale_grad: float32 [896], replicated
- gains_grad: float32 [4, 896], replicated
Inputs may be any that keep to these rules, and one draw needn't show every extreme that they name: Document lengths of each index of dp; they sum to 128, and the longest is 64. `query_codes`: whole numbers. `key_codes`: whole numbers. `value_codes`: whole numbers. `output_codes`: whole numbers. `gate_codes`: whole numbers. `upward_codes`: whole numbers. `down_codes`: whole numbers. `query_scale`: positive. `key_scale`: positive. `value_scale`: positive. `output_scale`: positive. `gate_scale`: positive. `upward_scale`: positive. `down_scale`: positive.
All inputs are finite; a program needn't handle non-finite values.
Results may differ from a plain program's by a relative error of at most 0.02.
Values may be sent and summed in bfloat16 or wider, within the bound.
A program may use at most 320 MiB of HBM per device.

v0:
```python
import jax
import jax.numpy as jnp
from jax import lax
from jax.sharding import PartitionSpec as P

HEAD_WIDTH = 64


EPS = 1e-06
CAP = 50.0
BASE = 10000.0
WIDTHS = (8, 4, 2)


def code_units(code_set, width_bits):
    bin_size = 2.0 ** (8 - width_bits)
    return bin_size * (
        jnp.floor(code_set.astype(jnp.float32) / bin_size) + 0.5 - 2.0 ** (width_bits - 1)
    )


def dequant(code_set, scale_row, width_bits):
    return (scale_row[None, :] * code_units(code_set, width_bits)).astype(jnp.bfloat16)


def product(left_side, right_side):
    return jnp.dot(left_side, right_side, preferred_element_type=jnp.float32)


def product_back(left_side, right_side):
    return lax.dot_general(
        left_side, right_side, (((1,), (1,)), ((), ())), preferred_element_type=jnp.float32
    )


def product_outer(left_side, right_side):
    return lax.dot_general(
        left_side, right_side, (((0,), (0,)), ((), ())), preferred_element_type=jnp.float32
    )


def rms_norm(tensor, gain_row):
    return tensor * lax.rsqrt(jnp.mean(tensor * tensor, axis=-1, keepdims=True) + EPS) * gain_row


def geglu(gate_value, upward):
    return jax.nn.gelu(gate_value, approximate=True) * upward


def doc_tables(lengths, count_of_rows):
    doc_ends = jnp.cumsum(lengths)
    starts = doc_ends - lengths
    token_ids = jnp.arange(count_of_rows, dtype=jnp.int32)
    segment = jnp.sum((token_ids[:, None] >= doc_ends[None, :]).astype(jnp.int32), axis=1)
    owners = segment[:, None] == jnp.arange(lengths.shape[0], dtype=jnp.int32)[None, :]
    token_position = token_ids - jnp.sum(jnp.where(owners, starts[None, :], 0), axis=1)
    allowed = (segment[:, None] == segment[None, :]) & (
        token_position[None, :] <= token_position[:, None]
    )
    return (token_position, allowed)


def rotary_apply(tensor, token_position, turning):
    head_size = tensor.shape[-1]
    half_size = head_size // 2
    inv_freq = BASE ** (-2.0 * jnp.arange(half_size, dtype=jnp.float32) / head_size)
    angles = token_position.astype(jnp.float32)[:, None] * inv_freq[None, :]
    cosine = jnp.cos(angles)[:, None, :]
    sines = turning * jnp.sin(angles)[:, None, :]
    first_half = tensor[..., :half_size]
    second_half = tensor[..., half_size:]
    return jnp.concatenate(
        [first_half * cosine - second_half * sines, second_half * cosine + first_half * sines],
        axis=-1,
    )


def attend_forward(query_rows, key_rows, value_rows, allowed):
    count_of_rows, kv_heads, head_size = key_rows.shape
    grouped_heads = query_rows.reshape(count_of_rows, kv_heads, -1, head_size)
    raw_scores = jnp.einsum(
        "qhgd,khd->hgqk", grouped_heads, key_rows, preferred_element_type=jnp.float32
    ) * head_size ** (-0.5)
    capped = jnp.where(allowed, CAP * jnp.tanh(raw_scores / CAP), -1e30)
    row_top = jnp.max(capped, axis=-1, keepdims=True)
    expos = jnp.exp(capped - row_top)
    row_total = jnp.sum(expos, axis=-1, keepdims=True)
    prob_rows = (expos / row_total).astype(jnp.bfloat16)
    mixed = jnp.einsum("hgqk,khd->qhgd", prob_rows, value_rows, preferred_element_type=jnp.float32)
    return (mixed.reshape(count_of_rows, -1), row_top + jnp.log(row_total))


def attend_back(query_rows, key_rows, value_rows, norm_log, grad_mixed, allowed):
    count_of_rows, kv_heads, head_size = key_rows.shape
    grouped_heads = query_rows.reshape(count_of_rows, kv_heads, -1, head_size)
    grad_rows = grad_mixed.reshape(grouped_heads.shape)
    factor = head_size ** (-0.5)
    raw_scores = (
        jnp.einsum("qhgd,khd->hgqk", grouped_heads, key_rows, preferred_element_type=jnp.float32)
        * factor
    )
    tanh_part = jnp.tanh(raw_scores / CAP)
    capped = jnp.where(allowed, CAP * tanh_part, -1e30)
    prob_rows = jnp.exp(capped - norm_log)
    grad_probs = jnp.einsum(
        "qhgd,khd->hgqk", grad_rows, value_rows, preferred_element_type=jnp.float32
    )
    grad_values = jnp.einsum(
        "hgqk,qhgd->khd",
        prob_rows.astype(jnp.bfloat16),
        grad_rows,
        preferred_element_type=jnp.float32,
    )
    grad_capped = prob_rows * (grad_probs - jnp.sum(grad_probs * prob_rows, axis=-1, keepdims=True))
    grad_raw = (grad_capped * (1.0 - tanh_part * tanh_part)).astype(jnp.bfloat16)
    grad_queries = (
        jnp.einsum("hgqk,khd->qhgd", grad_raw, key_rows, preferred_element_type=jnp.float32)
        * factor
    )
    grad_keys = (
        jnp.einsum("hgqk,qhgd->khd", grad_raw, grouped_heads, preferred_element_type=jnp.float32)
        * factor
    )
    return (grad_queries.reshape(count_of_rows, -1, head_size), grad_keys, grad_values)


def fold_widths(pieces, code_set):
    total = pieces[0] + pieces[1] + pieces[2]
    weighted = (
        pieces[0] * code_units(code_set, 8)
        + pieces[1] * code_units(code_set, 4)
        + pieces[2] * code_units(code_set, 2)
    )
    return (total, jnp.sum(weighted, axis=0))


def local(
    hidden_in,
    cotangent,
    lengths,
    gains,
    query_codes,
    key_codes,
    value_codes,
    output_codes,
    gate_codes,
    upward_codes,
    down_codes,
    query_scale,
    key_scale,
    value_scale,
    output_scale,
    gate_scale,
    upward_scale,
    down_scale,
):
    scales = (
        query_scale,
        key_scale,
        value_scale,
        output_scale,
        gate_scale,
        upward_scale,
        down_scale,
    )
    code_set = (
        lax.all_gather(query_codes, "dp", axis=0, tiled=True),
        lax.all_gather(key_codes, "dp", axis=0, tiled=True),
        lax.all_gather(value_codes, "dp", axis=0, tiled=True),
        lax.all_gather(output_codes, "dp", axis=1, tiled=True),
        lax.all_gather(gate_codes, "dp", axis=0, tiled=True),
        lax.all_gather(upward_codes, "dp", axis=0, tiled=True),
        lax.all_gather(down_codes, "dp", axis=1, tiled=True),
    )
    count_of_rows = hidden_in.shape[0]
    token_position, allowed = doc_tables(lengths[0], count_of_rows)
    inputs = hidden_in.astype(jnp.float32)
    normed_input, first_pull = jax.vjp(rms_norm, inputs, gains[0])
    normed_low = normed_input.astype(jnp.bfloat16)
    stored = []
    attention_parts = []
    for width_bits in WIDTHS:
        query_weight = dequant(code_set[0], scales[0], width_bits)
        key_matrix = dequant(code_set[1], scales[1], width_bits)
        value_matrix = dequant(code_set[2], scales[2], width_bits)
        output_weight = dequant(code_set[3], scales[3], width_bits)
        query_rows = rotary_apply(
            product(normed_low, query_weight).reshape(count_of_rows, -1, HEAD_WIDTH),
            token_position,
            1.0,
        ).astype(jnp.bfloat16)
        key_rows = rotary_apply(
            product(normed_low, key_matrix).reshape(count_of_rows, -1, HEAD_WIDTH),
            token_position,
            1.0,
        ).astype(jnp.bfloat16)
        value_rows = (
            product(normed_low, value_matrix)
            .astype(jnp.bfloat16)
            .reshape(count_of_rows, -1, HEAD_WIDTH)
        )
        mixed, norm_log = attend_forward(query_rows, key_rows, value_rows, allowed)
        mixed_low = mixed.astype(jnp.bfloat16)
        attention_parts.append(product(mixed_low, output_weight))
        stored.append((query_rows, key_rows, value_rows, norm_log, mixed_low))
    attention_total = lax.psum(jnp.stack(attention_parts), "mp")

    def second(hidden_rows, branch, gain_one, gain_two):
        lifted = hidden_rows[None] + rms_norm(branch, gain_one)
        return (lifted, rms_norm(lifted, gain_two))

    (lifted, normed_two), second_pull = jax.vjp(second, inputs, attention_total, gains[1], gains[2])
    normed_two_low = normed_two.astype(jnp.bfloat16)
    feed_stored = []
    feed_parts = []
    for number, width_bits in enumerate(WIDTHS):
        gate_weight = dequant(code_set[4], scales[4], width_bits)
        upward_weight = dequant(code_set[5], scales[5], width_bits)
        down_weight = dequant(code_set[6], scales[6], width_bits)
        gate_value = product(normed_two_low[number], gate_weight)
        upward = product(normed_two_low[number], upward_weight)
        activated = geglu(gate_value, upward).astype(jnp.bfloat16)
        feed_parts.append(product(activated, down_weight))
        feed_stored.append((gate_value, upward, activated))
    feed_total = lax.psum(jnp.stack(feed_parts).astype(jnp.bfloat16), "mp").astype(jnp.float32)

    def third(lifted_rows, branch, gain_row):
        return lifted_rows + rms_norm(branch, gain_row)

    result, third_pull = jax.vjp(third, lifted, feed_total, gains[3])
    grad_lifted, grad_feed, grad_gain_four = third_pull(cotangent.astype(jnp.float32))
    grad_feed_low = grad_feed.astype(jnp.bfloat16)
    code_set = (
        lax.all_gather(query_codes, "dp", axis=0, tiled=True),
        lax.all_gather(key_codes, "dp", axis=0, tiled=True),
        lax.all_gather(value_codes, "dp", axis=0, tiled=True),
        lax.all_gather(output_codes, "dp", axis=1, tiled=True),
        lax.all_gather(gate_codes, "dp", axis=0, tiled=True),
        lax.all_gather(upward_codes, "dp", axis=0, tiled=True),
        lax.all_gather(down_codes, "dp", axis=1, tiled=True),
    )
    grad_two_parts = []
    down_pieces = []
    gate_pieces = []
    upward_pieces = []
    for number, width_bits in enumerate(WIDTHS):
        gate_weight = dequant(code_set[4], scales[4], width_bits)
        upward_weight = dequant(code_set[5], scales[5], width_bits)
        down_weight = dequant(code_set[6], scales[6], width_bits)
        gate_value, upward, activated = feed_stored[number]
        grad_act = product_back(grad_feed_low[number], down_weight)
        down_pieces.append(product_outer(activated, grad_feed_low[number]))
        _, act_pull = jax.vjp(geglu, gate_value, upward)
        grad_gate, grad_upward = act_pull(grad_act)
        grad_gate = grad_gate.astype(jnp.bfloat16)
        grad_upward = grad_upward.astype(jnp.bfloat16)
        grad_two_parts.append(
            product_back(grad_gate, gate_weight) + product_back(grad_upward, upward_weight)
        )
        gate_pieces.append(product_outer(normed_two_low[number], grad_gate))
        upward_pieces.append(product_outer(normed_two_low[number], grad_upward))
    down_total, down_scale_part = fold_widths(down_pieces, code_set[6])
    gate_total, gate_scale_grad = fold_widths(gate_pieces, code_set[4])
    upward_total, upward_scale_grad = fold_widths(upward_pieces, code_set[5])
    grad_two, down_scale_grad = (
        lax.psum(jnp.stack(grad_two_parts).astype(jnp.bfloat16), "mp").astype(jnp.float32),
        lax.psum(down_scale_part.astype(jnp.bfloat16), "mp").astype(jnp.float32),
    )
    grad_inputs_two, grad_branch, grad_gain_two, grad_gain_three = second_pull(
        (grad_lifted, grad_two)
    )
    grad_branch_low = grad_branch.astype(jnp.bfloat16)
    grad_one_part = jnp.zeros(normed_input.shape, jnp.float32)
    query_pieces = []
    key_pieces = []
    value_pieces = []
    output_pieces = []
    for number, width_bits in enumerate(WIDTHS):
        query_weight = dequant(code_set[0], scales[0], width_bits)
        key_matrix = dequant(code_set[1], scales[1], width_bits)
        value_matrix = dequant(code_set[2], scales[2], width_bits)
        output_weight = dequant(code_set[3], scales[3], width_bits)
        query_rows, key_rows, value_rows, norm_log, mixed_low = stored[number]
        grad_mixed = product_back(grad_branch_low[number], output_weight).astype(jnp.bfloat16)
        output_pieces.append(product_outer(mixed_low, grad_branch_low[number]))
        grad_queries, grad_keys, grad_values = attend_back(
            query_rows, key_rows, value_rows, norm_log, grad_mixed, allowed
        )
        grad_queries = (
            rotary_apply(grad_queries, token_position, -1.0)
            .reshape(count_of_rows, -1)
            .astype(jnp.bfloat16)
        )
        grad_keys = (
            rotary_apply(grad_keys, token_position, -1.0)
            .reshape(count_of_rows, -1)
            .astype(jnp.bfloat16)
        )
        grad_values = grad_values.reshape(count_of_rows, -1).astype(jnp.bfloat16)
        grad_one_part = (
            grad_one_part
            + product_back(grad_queries, query_weight)
            + product_back(grad_keys, key_matrix)
            + product_back(grad_values, value_matrix)
        )
        query_pieces.append(product_outer(normed_low, grad_queries))
        key_pieces.append(product_outer(normed_low, grad_keys))
        value_pieces.append(product_outer(normed_low, grad_values))
    query_total, query_scale_grad = fold_widths(query_pieces, code_set[0])
    key_total, key_scale_grad = fold_widths(key_pieces, code_set[1])
    value_total, value_scale_grad = fold_widths(value_pieces, code_set[2])
    output_total, output_scale_part = fold_widths(output_pieces, code_set[3])
    grad_one, output_scale_grad = (
        lax.psum(grad_one_part.astype(jnp.bfloat16), "mp").astype(jnp.float32),
        lax.psum(output_scale_part.astype(jnp.bfloat16), "mp").astype(jnp.float32),
    )
    grad_inputs_one, grad_gain_one = first_pull(grad_one)
    input_grad = (grad_inputs_one + grad_inputs_two).astype(jnp.bfloat16)
    gains_part = jnp.stack([grad_gain_one, grad_gain_two, grad_gain_three, grad_gain_four])
    query_grad, key_grad, value_grad, output_grad, gate_grad, upward_grad, down_grad = (
        lax.psum_scatter(query_total, "dp", scatter_dimension=0, tiled=True),
        lax.psum_scatter(key_total, "dp", scatter_dimension=0, tiled=True),
        lax.psum_scatter(value_total, "dp", scatter_dimension=0, tiled=True),
        lax.psum_scatter(output_total, "dp", scatter_dimension=1, tiled=True),
        lax.psum_scatter(gate_total, "dp", scatter_dimension=0, tiled=True),
        lax.psum_scatter(upward_total, "dp", scatter_dimension=0, tiled=True),
        lax.psum_scatter(down_total, "dp", scatter_dimension=1, tiled=True),
    )
    small_set = lax.psum(
        (
            query_scale_grad,
            key_scale_grad,
            value_scale_grad,
            output_scale_grad,
            gate_scale_grad,
            upward_scale_grad,
            down_scale_grad,
            gains_part,
        ),
        "dp",
    )
    return (
        result.astype(jnp.bfloat16),
        input_grad,
        query_grad,
        key_grad,
        value_grad,
        output_grad,
        gate_grad,
        upward_grad,
        down_grad,
        small_set[0],
        small_set[1],
        small_set[2],
        small_set[3],
        small_set[4],
        small_set[5],
        small_set[6],
        small_set[7],
    )


def solution(mesh):
    placed = (
        P("dp", None),
        P(None, "dp", None),
        P("dp", None),
        P(),
        P("dp", "mp"),
        P("dp", "mp"),
        P("dp", "mp"),
        P("mp", "dp"),
        P("dp", "mp"),
        P("dp", "mp"),
        P("mp", "dp"),
        P("mp"),
        P("mp"),
        P("mp"),
        P(),
        P("mp"),
        P("mp"),
        P(),
    )
    return jax.shard_map(
        local,
        mesh=mesh,
        in_specs=placed,
        out_specs=(
            P(None, "dp", None),
            P("dp", None),
            P("dp", "mp"),
            P("dp", "mp"),
            P("dp", "mp"),
            P("mp", "dp"),
            P("dp", "mp"),
            P("dp", "mp"),
            P("mp", "dp"),
            P("mp"),
            P("mp"),
            P("mp"),
            P(),
            P("mp"),
            P("mp"),
            P(),
            P(),
        ),
        check_vma=False,
    )
```

profile of v0, /device:TPU:0, one launch (start us, length us, event | category | flops | bytes accessed | tf_op | source)
XLA Modules:
  0.0 2047.8 jit_solution(13292451537042186648)
XLA Ops:
  8.1 179.7 %all-gather = bf16[64,14,64]{2,1,0:T(8,128)(2,1)S(1)} all-gather(bf16[1,14,64]{2,1,0:T(8,128)(2,1)} %bitcast.588), channel_id=1, replica_groups=mesh['dp'=64,'mp'=2] {'dp'}, dimensions={0}, use_global_device_ids=true | all-gather | bytes 116480 | tf_op jit(solution)/shard_map/all_gather | solution.py:169
  190.6 175.1 %all-gather.2 = bf16[64,14,448]{2,1,0:T(8,128)(2,1)S(1)} all-gather(bf16[1,14,448]{2,1,0:T(8,128)(2,1)S(1)} %bitcast.586), channel_id=1, replica_groups=mesh['dp'=64,'mp'=2] {'dp'}, dimensions={0}, use_global_device_ids=true | all-gather | bytes 815360 | tf_op jit(solution)/shard_map/all_gather | solution.py:167
  374.8 172.2 %all-gather.1 = bf16[64,14,64]{2,1,0:T(8,128)(2,1)S(1)} all-gather(bf16[1,14,64]{2,1,0:T(8,128)(2,1)S(1)} %bitcast.589), channel_id=1, replica_groups=mesh['dp'=64,'mp'=2] {'dp'}, dimensions={0}, use_global_device_ids=true | all-gather | bytes 116480 | tf_op jit(solution)/shard_map/all_gather | solution.py:168
  553.9 175.2 %all-gather.3 = bf16[64,14,448]{2,1,0:T(8,128)(2,1)S(1)} all-gather(bf16[1,14,448]{2,1,0:T(8,128)(2,1)S(1)} %bitcast.587), channel_id=1, replica_groups=mesh['dp'=64,'mp'=2] {'dp'}, dimensions={0}, use_global_device_ids=true | all-gather | bytes 815360 | tf_op jit(solution)/shard_map/all_gather | solution.py:170
  766.5 18.7 all-reduce.19.cloned.1.call-done
  789.2 44.2 %all-gather.11.cloned.1.call-done = bf16[64,14,2432]{2,1,0:T(8,128)(2,1)} async-done(((bf16[1,14,2432]{2,1,0:T(8,128)(2,1)}), bf16[64,14,2432]{2,1,0:T(8,128)(2,1)}) %all-gather.11.cloned.1.call-update) | async-done | bytes 4358160 | tf_op jit(solution)/shard_map/all_gather | solution.py:171
  833.5 12.3 fusion.4
  845.8 9.6 reshape.782
  855.4 49.1 %all-gather.13.cloned.1.call-done = bf16[64,14,2432]{2,1,0:T(8,128)(2,1)} async-done(((bf16[1,14,2432]{2,1,0:T(8,128)(2,1)}), bf16[64,14,2432]{2,1,0:T(8,128)(2,1)}) %all-gather.13.cloned.1.call-update) | async-done | bytes 4358160 | tf_op jit(solution)/shard_map/all_gather | solution.py:172
  904.5 12.3 fusion.9
  916.8 9.6 reshape.784
  926.4 49.1 %all-gather.15.cloned.1.call-done = bf16[64,14,2432]{2,1,0:T(8,128)(2,1)} async-done(((bf16[1,14,2432]{2,1,0:T(8,128)(2,1)}), bf16[64,14,2432]{2,1,0:T(8,128)(2,1)}) %all-gather.15.cloned.1.call-update) | async-done | bytes 4358160 | tf_op jit(solution)/shard_map/all_gather | solution.py:173
  975.5 12.1 fusion.13
  987.6 9.6 reshape.792
  997.2 10.6 copy.139
  1007.8 9.6 reshape.778
  1017.4 9.6 reshape.780
  1027.0 9.6 reshape.791
  1036.6 10.6 copy.138
  1047.2 9.6 reshape.748
  1056.8 9.6 reshape.750
  1066.4 9.6 reshape.790
  1076.0 11.0 copy.137
  1087.0 4.5 fusion.36
  1091.6 4.8 fusion.44
  1096.4 6.6 fusion.40
  1136.8 3.7 all-reduce.21.cloned.1.call-done
  1145.6 5.0 fusion.203
  1150.6 5.7 fusion.202
  1160.8 5.8 fusion.211
  1169.9 4.9 fusion.209
  1174.9 5.7 multiply_convert_fusion.22
  1190.6 21.0 %fusion.18 = (bf16[896]{0:T(1024)(128)(2,1)S(1)}, f32[2432,896]{1,0:T(8,128)}) fusion(f32[2432,896]{1,0:T(8,128)} %fusion.203, f32[2432,896]{1,0:T(8,128)} %fusion.202, f32[896,2432]{0,1:T(8,128)} %copy.137, f32[896,2432]{0,1:T(8,128)} %copy.139, f32[896,2432]{0,1:T(8,128)} %copy.138, bf16[128,2432]{1,0:T(8,128)(2,1)} %copy-done.44, ...), kind=kOutput, calls=%fused_computation.27 | convolution fusion | flops 583990400 | bytes 53151488 | tf_op jit(solution)/shard_map/dot_general | solution.py:37
  1211.5 20.4 add_reduce_fusion.1
  1231.9 5.8 fusion.210
  1237.7 5.7 fusion.208
  1271.6 5.1 fusion.54
  1283.2 19.0 add_reduce_fusion
  1302.2 294.9 %fusion.320 = (f32[16,2432]{1,0:T(8,128)S(1)}, f32[16,2432]{1,0:T(8,128)S(1)}) fusion(f32[896,2432]{1,0:T(8,128)} %get-tuple-element.127, f32[896,2432]{1,0:T(8,128)} %get-tuple-element.125), kind=kCustom, calls=%all-reduce-scatter.2 | all-reduce-scatter fusion | flops 4980737 | bytes 17744384
  1607.5 5.6 collective-permute-done.15
  1619.4 8.0 collective-permute-start.14
  1627.4 4.8 collective-permute-start.13
  1632.2 6.1 collective-permute-start.12
  1638.3 6.1 collective-permute-start.11
  1644.4 6.7 collective-permute-start.10
  1651.1 7.4 collective-permute-start.9
  1665.8 14.5 concatenate.100
  1686.3 342.1 %all-reduce.9 = (f32[448]{0:T(512)}, f32[64]{0:T(128)}, f32[64]{0:T(128)}, f32[896]{0:T(1024)}, f32[2432]{0:T(1024)}, /*index=5*/f32[2432]{0:T(1024)}, f32[896]{0:T(1024)}, f32[4,896]{1,0:T(4,128)}) all-reduce(f32[448]{0:T(512)S(1)} %get-tuple-element.141, f32[64]{0:T(128)S(1)} %get-tuple-element.159, ...), channel_id=1, replica_groups=mesh['dp'=64,'mp'=2] {'dp'}, use_global_device_ids=true, to_apply=%region_33.34 | all-reduce | flops 10816 | bytes 82944 | tf_op jit(solution)/shard_map/psum | solution.py:329
  (666 shorter events, 189.5 us)
Async XLA Ops:
  8.0 181.7 %copy-start.164 = (f32[64]{0:T(128)S(1)}, f32[64]{0:T(128)}, u32[]{:S(2)}) copy-start(f32[64]{0:T(128)} %param.31) | copy-start | bytes 772
  8.0 181.7 %copy-start.156 = (f32[4,896]{1,0:T(4,128)S(1)}, f32[4,896]{1,0:T(4,128)}, u32[]{:S(2)}) copy-start(f32[4,896]{1,0:T(4,128)} %param.21) | copy-start | bytes 43012
  8.0 182.3 %copy-start = (bf16[128,896]{1,0:T(8,128)(2,1)S(1)}, bf16[128,896]{1,0:T(8,128)(2,1)}, u32[]{:S(2)}) copy-start(bf16[128,896]{1,0:T(8,128)(2,1)} %param.18) | copy-start | bytes 688132
  8.1 777.1 %all-reduce.19.cloned.1.call-start = ((), (), s32[]{:S(2)}) async-start(), calls=%async_computation | async-start | bytes 2752512 | tf_op jit(solution)/shard_map/psum | solution.py:206
  8.1 748.4 %copy-start.157 = (f32[32]{0:T(128)}, f32[32]{0:T(128)S(1)}, u32[]{:S(2)}) copy-start(f32[32]{0:T(128)S(1)} %multiply_power_fusion) | copy-start | bytes 388
  189.8 562.3 %copy-start.173 = (f32[64]{0:T(128)}, f32[64]{0:T(128)S(1)}, u32[]{:S(2)}) copy-start(f32[64]{0:T(128)S(1)} %get-tuple-element.226) | copy-start | bytes 772
  189.8 568.8 %copy-start.166 = (f32[64]{0:T(128)}, f32[64]{0:T(128)S(1)}, u32[]{:S(2)}) copy-start(f32[64]{0:T(128)S(1)} %get-tuple-element.225) | copy-start | bytes 772
  190.4 568.1 %copy-start.64 = (f32[896]{0:T(1024)}, f32[896]{0:T(1024)S(1)}, u32[]{:S(2)}) copy-start(f32[896]{0:T(1024)S(1)} %get-tuple-element.103) | copy-start | bytes 10756
  190.4 597.5 %copy-start.107 = (f32[896]{0:T(1024)}, f32[896]{0:T(1024)S(1)}, u32[]{:S(2)}) copy-start(f32[896]{0:T(1024)S(1)} %get-tuple-element.102) | copy-start | bytes 10756
  190.4 597.5 %copy-start.111 = (f32[896]{0:T(1024)}, f32[896]{0:T(1024)S(1)}, u32[]{:S(2)}) copy-start(f32[896]{0:T(1024)S(1)} %get-tuple-element.104) | copy-start | bytes 10756
  190.5 178.0 %copy-start.175 = (f32[128]{0:T(128)}, f32[128]{0:T(128)S(1)}, u32[]{:S(2)}) copy-start(f32[128]{0:T(128)S(1)} %multiply_reduce_fusion.7) | copy-start | bytes 1540
  190.5 568.0 %copy-start.100 = (f32[128]{0:T(128)}, f32[128]{0:T(128)S(1)}, u32[]{:S(2)}) copy-start(f32[128]{0:T(128)S(1)} %fusion.276) | copy-start | bytes 1540
  371.5 385.0 %copy-start.159 = (f32[128]{0:T(128)}, f32[128]{0:T(128)S(1)}, u32[]{:S(2)}) copy-start(f32[128]{0:T(128)S(1)} %get-tuple-element.228) | copy-start | bytes 1540
  373.1 380.1 %copy-start.149 = (f32[448]{0:T(512)}, f32[448]{0:T(512)S(1)}, u32[]{:S(2)}) copy-start(f32[448]{0:T(512)S(1)} %get-tuple-element.210) | copy-start | bytes 5380
  373.1 382.1 %copy-start.147 = (f32[448]{0:T(512)}, f32[448]{0:T(512)S(1)}, u32[]{:S(2)}) copy-start(f32[448]{0:T(512)S(1)} %get-tuple-element.211) | copy-start | bytes 5380
  374.8 173.4 %copy-start.162 = (f32[64]{0:T(128)S(1)}, f32[64]{0:T(128)}, u32[]{:S(2)}) copy-start(f32[64]{0:T(128)} %param.30) | copy-start | bytes 772
  548.2 207.5 %copy-start.168 = (f32[64]{0:T(128)}, f32[64]{0:T(128)S(1)}, u32[]{:S(2)}) copy-start(f32[64]{0:T(128)S(1)} %get-tuple-element.230) | copy-start | bytes 772
  548.2 207.8 %copy-start.170 = (f32[64]{0:T(128)}, f32[64]{0:T(128)S(1)}, u32[]{:S(2)}) copy-start(f32[64]{0:T(128)S(1)} %get-tuple-element.229) | copy-start | bytes 772
  551.8 204.0 %copy-start.25 = (f32[896,64]{1,0:T(8,128)}, f32[896,64]{1,0:T(8,128)S(1)}, u32[]{:S(2)}) copy-start(f32[896,64]{1,0:T(8,128)S(1)} %reshape.774) | copy-start | bytes 688132
  553.9 205.9 %copy-start.90 = (pred[128,128]{0,1:T(8,128)(4,1)}, pred[128,128]{0,1:T(8,128)(4,1)S(1)}, u32[]{:S(2)}) copy-start(pred[128,128]{0,1:T(8,128)(4,1)S(1)} %compare_and_fusion) | copy-start | bytes 49156
  764.4 69.1 %all-gather.11.cloned.1.call-start = ((), (), s32[]{:S(2)}) async-start(), calls=%async_computation.4 | async-start | bytes 5058560 | tf_op jit(solution)/shard_map/all_gather | solution.py:171
  765.0 139.5 %all-gather.13.cloned.1.call-start = ((), (), s32[]{:S(2)}) async-start(), calls=%async_computation.5 | async-start | bytes 5058560 | tf_op jit(solution)/shard_map/all_gather | solution.py:172
  765.6 209.9 %all-gather.15.cloned.1.call-start = ((), (), s32[]{:S(2)}) async-start(), calls=%async_computation.6 | async-start | bytes 5058560 | tf_op jit(solution)/shard_map/all_gather | solution.py:173
  766.1 374.4 %all-reduce.21.cloned.1.call-start = ((), (), s32[]{:S(2)}) async-start(), calls=%async_computation.1 | async-start | bytes 1376256 | tf_op jit(solution)/shard_map/psum | solution.py:225
  787.8 58.0 %copy-start.145 = (f32[3,128]{1,0:T(4,128)}, f32[3,128]{1,0:T(4,128)S(1)}, u32[]{:S(2)}) copy-start(f32[3,128]{1,0:T(4,128)S(1)} %multiply_reduce_fusion.2) | copy-start | bytes 4612
  789.2 442.7 %copy-start.13 = (bf16[3,128,896]{2,1,0:T(8,128)(2,1)}, bf16[3,128,896]{2,1,0:T(8,128)(2,1)S(1)}, u32[]{:S(2)}) copy-start(bf16[3,128,896]{2,1,0:T(8,128)(2,1)S(1)} %multiply_convert_fusion.21) | copy-start | bytes 2064388
  1118.2 125.3 %all-reduce.23.cloned.1.call-start = ((), (), s32[]{:S(2)}) async-start(), calls=%async_computation.2 | async-start | bytes 1376256 | tf_op jit(solution)/shard_map/psum | solution.py:266
  1190.1 494.9 %all-reduce.25.cloned.1.call-start = ((), (), s32[]{:S(2)}) async-start(), calls=%async_computation.3 | async-start | bytes 458752 | tf_op jit(solution)/shard_map/psum | solution.py:314
  1271.5 758.7 %all-reduce.27.cloned.1.call-start = ((), (), s32[]{:S(2)}) async-start(), calls=%async_computation.7 | async-start | bytes 24772608
  1302.2 358.2 %copy-start.172 = (u32[128]{0:T(128)S(1)}, u32[128]{0:T(128)}, u32[]{:S(2)}) copy-start(u32[128]{0:T(128)} %constant.173) | copy-start | bytes 1540
  1597.1 6.8 collective-permute-start.7
  1598.4 16.2 collective-permute-start.6
  1599.7 17.1 collective-permute-start.5
  1601.0 18.3 collective-permute-start.4
  1602.3 25.0 %collective-permute-start.3 = (f32[16,2432]{1,0:T(8,128)S(1)}, f32[16,2432]{1,0:T(8,128)S(1)}, u32[]{:S(2)}, u32[]{:S(2)}) collective-permute-start(f32[16,2432]{1,0:T(8,128)S(1)} %get-tuple-element.122), channel_id=1, source_target_pairs={{0,8},{2,10},{4,12},{6,14},{8,16},{10,18},{12,20},{14,22},{16,24},... | collective-permute-start | bytes 466952
  1603.9 9.1 collective-permute-start.15
  1613.0 19.2 collective-permute-start.2
  1614.6 23.7 %collective-permute-start.1 = (f32[16,2432]{1,0:T(8,128)S(1)}, f32[16,2432]{1,0:T(8,128)S(1)}, u32[]{:S(2)}, u32[]{:S(2)}) collective-permute-start(f32[16,2432]{1,0:T(8,128)S(1)} %get-tuple-element.122), channel_id=1, source_target_pairs={{0,4},{2,6},{4,8},{6,10},{8,12},{10,14},{12,16},{14,18},{16,20},{1... | collective-permute-start | bytes 466952
  1616.8 27.6 %collective-permute-start = (f32[16,2432]{1,0:T(8,128)S(1)}, f32[16,2432]{1,0:T(8,128)S(1)}, u32[]{:S(2)}, u32[]{:S(2)}) collective-permute-start(f32[16,2432]{1,0:T(8,128)S(1)} %get-tuple-element.122), channel_id=1, source_target_pairs={{0,2},{2,4},{4,6},{6,8},{8,10},{10,12},{12,14},{14,16},{16,18},{18... | collective-permute-start | bytes 466952
  1619.4 31.7 %collective-permute-start.14 = (f32[16,2432]{1,0:T(8,128)S(1)}, f32[16,2432]{1,0:T(8,128)S(1)}, u32[]{:S(2)}, u32[]{:S(2)}) collective-permute-start(f32[16,2432]{1,0:T(8,128)S(1)} %get-tuple-element.123), channel_id=1, source_target_pairs={{0,14},{2,16},{4,18},{6,20},{8,22},{10,24},{12,26},{14,28},{16,30}... | collective-permute-start | bytes 466952
  1627.4 31.1 %collective-permute-start.13 = (f32[16,2432]{1,0:T(8,128)S(1)}, f32[16,2432]{1,0:T(8,128)S(1)}, u32[]{:S(2)}, u32[]{:S(2)}) collective-permute-start(f32[16,2432]{1,0:T(8,128)S(1)} %get-tuple-element.123), channel_id=1, source_target_pairs={{0,12},{2,14},{4,16},{6,18},{8,20},{10,22},{12,24},{14,26},{16,28}... | collective-permute-start | bytes 466952
  1632.2 33.5 %collective-permute-start.12 = (f32[16,2432]{1,0:T(8,128)S(1)}, f32[16,2432]{1,0:T(8,128)}, u32[]{:S(2)}, u32[]{:S(2)}) collective-permute-start(f32[16,2432]{1,0:T(8,128)S(1)} %get-tuple-element.123), channel_id=1, source_target_pairs={{0,10},{2,12},{4,14},{6,16},{8,18},{10,20},{12,22},{14,24},{16,26}... | collective-permute-start | bytes 466952
  1638.3 27.4 %collective-permute-start.11 = (f32[16,2432]{1,0:T(8,128)S(1)}, f32[16,2432]{1,0:T(8,128)}, u32[]{:S(2)}, u32[]{:S(2)}) collective-permute-start(f32[16,2432]{1,0:T(8,128)S(1)} %get-tuple-element.123), channel_id=1, source_target_pairs={{0,8},{2,10},{4,12},{6,14},{8,16},{10,18},{12,20},{14,22},{16,24},... | collective-permute-start | bytes 466952
  1644.4 21.4 %collective-permute-start.10 = (f32[16,2432]{1,0:T(8,128)S(1)}, f32[16,2432]{1,0:T(8,128)}, u32[]{:S(2)}, u32[]{:S(2)}) collective-permute-start(f32[16,2432]{1,0:T(8,128)S(1)} %get-tuple-element.123), channel_id=1, source_target_pairs={{0,6},{2,8},{4,10},{6,12},{8,14},{10,16},{12,18},{14,20},{16,22},{... | collective-permute-start | bytes 466952
  1651.1 14.7 collective-permute-start.9
  1658.5 7.3 collective-permute-start.8
  1665.7 362.6 %copy-start.176 = (f32[128]{0:T(128)S(1)}, f32[128]{0:T(128)}, u32[]{:S(2)}) copy-start(f32[128]{0:T(128)} %copy-done.175) | copy-start | bytes 1540
  1665.7 362.6 %copy-start.61 = (f32[128,896]{1,0:T(8,128)S(1)}, f32[128,896]{1,0:T(8,128)}, u32[]{:S(2)}) copy-start(f32[128,896]{1,0:T(8,128)} %get-tuple-element.86) | copy-start | bytes 1376260
  (196 other events, 912.1 us)
Sparse Core Ops, SparseCore 0:
  764.5 20.6 all-reduce.18
  1118.3 22.1 all-reduce.20
  1190.3 25.9 all-reduce.22
  1271.6 25.0 all-reduce.24
  1304.0 398.0 all-reduce.26
Sparse Core Ops, SparseCore 1:
  768.1 65.3 all-gather.10
  836.6 67.8 all-gather.12
  907.6 67.8 all-gather.14
where the time goes:
time: 2060 us; the launch traced here: 2050 us
  blocking collectives  1340 us (65%)
  local copies, waits for them, and re-layouts  214 us (10%)
  matrix products  173 us (8%)
  waiting for transfers between devices  172 us (8%)
  other arithmetic  67.9 us (3%)
  starting transfers between devices  58.5 us (3%)
    psum x1, blocking collectives, local(): lax.psum((query_scale_grad, key_scale_grad, value_scale_grad, output_scal...  342 us
    unnamed x1, blocking collectives  295 us
    all_gather x1, blocking collectives, local(): lax.all_gather(value_codes, 'dp', axis=0, tiled=True)  180 us
    all_gather x1, blocking collectives, local(): lax.all_gather(output_codes, 'dp', axis=1, tiled=True)  175 us
    all_gather x1, blocking collectives, local(): lax.all_gather(query_codes, 'dp', axis=0, tiled=True)  175 us
    all_gather x1, blocking collectives, local(): lax.all_gather(key_codes, 'dp', axis=0, tiled=True)  172 us
    sub x28, local copies, waits for them, and re-layouts, code_units(): jnp.floor(code_set.astype(jnp.float32) / bin_size) + 0.5  115 us
    dot_general x21, matrix products, product_outer(): lax.dot_general(left_side, right_side, (((0,), (0,)), ((), ())), preferre...  113 us
  transfers between devices with their start and end apart: 24, of which 6 were waited for; matrix products, arithmetic and copies ran while one was open for 23% of the time, Pallas kernels for 0%

commit v1 on v0

v1 whole, which is shorter than its diff:
```python
import functools
import math

import jax
import jax.numpy as jnp
from jax import lax
from jax.experimental import pallas as pl
from jax.experimental.pallas import tpu as pltpu
from jax.sharding import PartitionSpec as P
MESH = pl.DeviceIdType.MESH
STRIDE = {"x": 16, "y": 4, "z": 1}
AX = "xyz"
ORDERS = ("zyx", "xzy", "yxz")

class Here:
    def __init__(s):
        s.dp = lax.axis_index("dp"); s.mp = lax.axis_index("mp")
        s.c = {a: lax.rem(s.dp // STRIDE[a], 4) for a in AX}
    def nbr(s, a, d):
        c = s.c[a]
        return (s.dp + (lax.rem(c + d, 4) - c) * STRIDE[a], s.mp)
    def at(s, a, d):
        return lax.rem(s.c[a] + d, 4)

def region(h, buf, slabs, order, phase, v):
    idx = {}
    for i, a in enumerate(order):
        idx[a] = slice(None) if i < phase else (v if i == phase else h.c[a])
    return buf.at[(slabs, idx["x"], idx["y"], idx["z"])]

def rcopy(src, dst, ss, rs, dev):
    return pltpu.make_async_remote_copy(src_ref=src, dst_ref=dst, send_sem=ss, recv_sem=rs, device_id=dev, device_id_type=MESH)

def barrier(h):
    b = pltpu.get_barrier_semaphore()
    for a in AX:
        for d in (1, 3):
            pl.semaphore_signal(b, inc=1, device_id=h.nbr(a, d), device_id_type=MESH)
    pl.semaphore_wait(b, 6)

def ring_A(h, buf, slabs, order, phase, ss, rs):
    a = order[phase]
    r = region(h, buf, slabs, order, phase, h.c[a])
    return [rcopy(r, r, ss.at[0], rs.at[0], h.nbr(a, 1)), rcopy(r, r, ss.at[1], rs.at[1], h.nbr(a, 3))]

def ring_B(h, buf, slabs, order, phase, ss, rs):
    a = order[phase]
    lo, n = slabs.start, slabs.size
    m = n // 2
    r0 = region(h, buf, pl.ds(lo, m), order, phase, h.at(a, 3))
    r1 = region(h, buf, pl.ds(lo + m, n - m), order, phase, h.at(a, 1))
    return [rcopy(r0, r0, ss.at[2], rs.at[2], h.nbr(a, 1)), rcopy(r1, r1, ss.at[3], rs.at[3], h.nbr(a, 3))]

def gather_body(nslab, groups, chunks3, s_ref, out_ref, lsem, ss, rs):
    h = Here()
    me = out_ref.at[:, h.c["x"], h.c["y"], h.c["z"]]
    cp = pltpu.make_async_copy(s_ref, me, lsem); cp.start()
    barrier(h)
    cp.wait()
    sends = []
    for phase in range(3):
        work = []
        for g, (lo, n) in enumerate(groups):
            if phase < 2:
                parts = [(lo, n)]
            else:
                parts = [(lo + a, b) for a, b in chunks3[g]]
            for k, (l, m) in enumerate(parts):
                work.append((g, k, pl.ds(l, m), ss.at[g, phase + k], rs.at[g, phase + k]))
        work.sort(key=lambda w: w[1])
        A = []; B = []
        for g, k, sl, s_, r_ in work:
            A.append(ring_A(h, out_ref, sl, ORDERS[g], phase, s_, r_))
            for c in A[-1]: c.start()
        for i, (g, k, sl, s_, r_) in enumerate(work):
            B.append(ring_B(h, out_ref, sl, ORDERS[g], phase, s_, r_))
            for j in range(2):
                A[i][j].wait_recv(); B[i][j].start()
        for b in B:
            for c in b: c.wait_recv()
        sends += [c for x in A + B for c in x]
    for c in sends: c.wait_send()

def gather(s, groups, chunks3, cid=0, space=pl.ANY):
    nslab = s.shape[0]
    nk = max(len(c) for c in chunks3)
    return pl.pallas_call(
        functools.partial(gather_body, nslab, groups, chunks3),
        out_shape=jax.ShapeDtypeStruct((nslab, 4, 4, 4, 16, 128), s.dtype),
        in_specs=[pl.BlockSpec(memory_space=space)], out_specs=pl.BlockSpec(memory_space=space),
        scratch_shapes=[pltpu.SemaphoreType.DMA, pltpu.SemaphoreType.DMA((3, 2 + nk, 4)), pltpu.SemaphoreType.DMA((3, 2 + nk, 4))],
        compiler_params=pltpu.CompilerParams(collective_id=cid, has_side_effects=True, vmem_limit_bytes=60 << 20),
    )(s)

def barrier9(h):
    b = pltpu.get_barrier_semaphore()
    for a in AX:
        for d in (1, 2, 3):
            pl.semaphore_signal(b, inc=1, device_id=h.nbr(a, d), device_id_type=MESH)
    pl.semaphore_wait(b, 9)

def idx_of(h, order, phase, v):
    idx = {}
    for i, a in enumerate(order):
        idx[a] = slice(None) if i < phase else (v if i == phase else h.c[a])
    return idx["x"], idx["y"], idx["z"]

class Scatter:
    def __init__(s, h, gv, r1, r2, order, phase, lo, n, ss, rs):
        s.__dict__.update(h=h, gv=gv, r1=r1, r2=r2, order=order, phase=phase, lo=lo, n=n)
        a = order[phase]
        s.right, s.left = h.nbr(a, 1), h.nbr(a, 3)
        m = n // 2
        s.h0, s.h1 = (lo, m), (lo + m, n - m)
        R = lambda part, d: gv.at[(pl.ds(*part),) + idx_of(h, order, phase, h.at(a, d))]
        s.first = [rcopy(R(s.h0, 2), r1.at[pl.ds(*s.h0)], ss.at[0], rs.at[0], s.right),
                   rcopy(R(s.h1, 2), r1.at[pl.ds(*s.h1)], ss.at[1], rs.at[1], s.left)]
        s.second = [rcopy(R(s.h1, 1), r2.at[0, pl.ds(*s.h1)], ss.at[2], rs.at[2], s.right),
                    rcopy(R(s.h0, 3), r2.at[1, pl.ds(*s.h0)], ss.at[3], rs.at[3], s.left)]
        s.third = [rcopy(R(s.h0, 1), r2.at[0, pl.ds(*s.h0)], ss.at[4], rs.at[4], s.right),
                   rcopy(R(s.h1, 3), r2.at[1, pl.ds(*s.h1)], ss.at[5], rs.at[5], s.left)]
    def start(s):
        for c in s.first + s.second: c.start()
    def add(s, part, d, srcs):
        ix = idx_of(s.h, s.order, s.phase, s.h.at(s.order[s.phase], d))
        @pl.loop(0, part[1])
        def _(i):
            k = part[0] + i
            t = s.gv[(k,) + ix].astype(jnp.float32)
            for r in srcs: t = t + r[k].astype(jnp.float32)
            s.gv[(k,) + ix] = t.astype(jnp.bfloat16)
    def relay(s):
        s.first[0].wait_recv(); s.add(s.h0, 1, [s.r1]); s.third[0].start()
        s.first[1].wait_recv(); s.add(s.h1, 3, [s.r1]); s.third[1].start()
    def finish(s):
        for c in s.second + s.third: c.wait_recv()
        s.add((s.lo, s.n), 0, [s.r2.at[0], s.r2.at[1]])
    def done(s):
        for c in s.first + s.second + s.third: c.wait_send()

def small_phase(h, a, slots, ss, rs):
    cs = [rcopy(slots.at[h.c[a]], slots.at[h.c[a]], ss.at[d - 1], rs.at[d - 1], h.nbr(a, d)) for d in (1, 2, 3)]
    return cs

def scatter_body(groups, chunks, g_ref, sm_ref, out_ref, smo_ref, gv, r1a, r2a, r1b, r2b, r1c, r2c, slots, lsem, ss, rs, sms, smr):
    h = Here()
    cp = pltpu.make_async_copy(g_ref, gv, lsem); cp.start()
    barrier9(h)
    cp.wait()
    cur = sm_ref[...]
    smc = []
    def small_start(p):
        slots[p, h.c[AX[p]]] = cur
        cs = small_phase(h, AX[p], slots.at[p], sms.at[p], smr.at[p])
        for c in cs: c.start()
        return cs
    def small_end(p, cs):
        for c in cs: c.wait_recv()
        smc.extend(cs)
        return (slots[p, 0] + slots[p, 1]) + (slots[p, 2] + slots[p, 3])
    done = []
    for i, (phase, r1, r2) in enumerate(((2, r1a, r2a), (1, r1b, r2b), (0, r1c, r2c))):
        work = []
        sc = small_start(i)
        for k in range(len(chunks[0]) if phase == 2 else 1):
            for g, (lo, n) in enumerate(groups):
                l, m = (lo + chunks[g][k][0], chunks[g][k][1]) if phase == 2 else (lo, n)
                work.append(Scatter(h, gv, r1, r2, ORDERS[g], phase, l, m, ss.at[g, (2 - phase) if phase < 2 else 3 + k], rs.at[g, (2 - phase) if phase < 2 else 3 + k]))
        for w in work: w.start()
        for w in work: w.relay()
        for w in work: w.finish()
        cur = small_end(i, sc)
        done += work
    smo_ref[...] = cur
    @pl.loop(0, out_ref.shape[0])
    def _(k):
        out_ref[k] = gv[k, h.c["x"], h.c["y"], h.c["z"]].astype(jnp.float32)
    for w in done: w.done()
    for c in smc: c.wait_send()

def scatter(g, sm, groups, chunks, cid=1):
    n = g.shape[0]; nk = max(len(c) for c in chunks)
    bf = jnp.bfloat16; V = pltpu.VMEM
    return pl.pallas_call(
        functools.partial(scatter_body, groups, chunks),
        out_shape=(jax.ShapeDtypeStruct((n, 16, 128), jnp.float32), jax.ShapeDtypeStruct(sm.shape, jnp.float32)),
        in_specs=[pl.BlockSpec(memory_space=pl.ANY), pl.BlockSpec(memory_space=V)],
        out_specs=(pl.BlockSpec(memory_space=V),) * 2,
        scratch_shapes=[V((n, 4, 4, 4, 16, 128), bf), V((n, 4, 4, 16, 128), bf), V((2, n, 4, 4, 16, 128), bf),
                        V((n, 4, 16, 128), bf), V((2, n, 4, 16, 128), bf), V((n, 16, 128), bf), V((2, n, 16, 128), bf),
                        V((3, 4) + sm.shape, jnp.float32),
                        pltpu.SemaphoreType.DMA, pltpu.SemaphoreType.DMA((3, 3 + nk, 6)), pltpu.SemaphoreType.DMA((3, 3 + nk, 6)),
                        pltpu.SemaphoreType.DMA((3, 3)), pltpu.SemaphoreType.DMA((3, 3))],
        compiler_params=pltpu.CompilerParams(collective_id=cid, has_side_effects=True, vmem_limit_bytes=60 << 20),
    )(g, sm)
F32, BF = jnp.float32, jnp.bfloat16
HI = lax.Precision.HIGHEST
MUL = (1.0, 16.0, 64.0)
OFF = (-127.5, -120.0, -96.0)
EPS, CAP = 1e-6, 50.0
GATE, UP, DOWN = 8, 27, 46
C0, C1 = math.sqrt(2 / math.pi), 0.044715

def nn(a, b): return lax.dot_general(a, b, (((1,), (0,)), ((), ())), preferred_element_type=F32)
def nt(a, b): return lax.dot_general(a, b, (((1,), (1,)), ((), ())), preferred_element_type=F32)
def tn(a, b): return lax.dot_general(a, b, (((0,), (0,)), ((), ())), preferred_element_type=F32)
def nt_hi(a, b): return lax.dot_general(a, b, (((1,), (1,)), ((), ())), preferred_element_type=F32, precision=HI)
def nn_hi(a, b): return lax.dot_general(a, b, (((1,), (0,)), ((), ())), preferred_element_type=F32, precision=HI)
def iota(s, d): return lax.broadcasted_iota(jnp.int32, s, d)
def rsum(a): return jnp.sum(a.astype(F32), axis=-1, keepdims=True)
def csum(a): return jnp.sum(a, axis=0, keepdims=True)

def spread_matrix():
    r, c = iota((896, 1024), 0), iota((896, 1024), 1)
    return jnp.where(c == r + 2 * lax.shift_right_logical(r * 4682, 16), 1.0, 0.0)

def units(c, b):
    if b == 0: return c
    return jnp.floor(c * BF(1 / MUL[b]))

def rinv(v): return lax.rsqrt(jnp.sum(v * v, axis=-1, keepdims=True) * (1 / 896) + EPS)
def rms_back(v, r, gain, dy):
    gd = gain * dy
    m = jnp.sum(v * gd, axis=-1, keepdims=True) * (1 / 896)
    return r * gd - v * (r * r * r * m), csum(dy * v * r)

class Comp:
    def __init__(s, **kw): s.__dict__.update(kw)
    def slab(s, k): return s.w[k].reshape(1024, 128)
    def codes(s, lo, n): return jnp.concatenate([s.slab(lo + i) for i in range(n)], axis=1)

    def exchange(s, k, part):
        n = part.shape[0]
        s.xs[k, pl.ds(0, n)] = part.astype(BF)
        c = rcopy(s.xs.at[k, pl.ds(0, n)], s.xr.at[k, pl.ds(0, n)], s.xss.at[k], s.xrs.at[k], (s.h.dp, 1 - s.h.mp))
        c.start(); c.wait()
        return s.xs[k, pl.ds(0, n)].astype(F32) + s.xr[k, pl.ds(0, n)].astype(F32)

    def prologue(s):
        p = spread_matrix()
        s.p[...] = p.astype(BF)
        s.gp[...] = nn_hi(s.gains[...], p)
        s.so[...] = nn_hi(s.o_scale[...], p)
        s.sd[...] = nn_hi(s.d_scale[...], p)
        s.hid[...] = nn(s.hidden[...], s.p[...])
        l0, l1 = s.lengths[0, 0], s.lengths[0, 1]
        def seg_of(i): return jnp.where(i >= l0, 1, 0) + jnp.where(i >= l0 + l1, 1, 0)
        ti, tj = iota((128, 128), 0), iota((128, 128), 1)
        si, sj = seg_of(ti), seg_of(tj)
        s.allow[...] = jnp.where((si == sj) & (tj <= ti), 1.0, 0.0)
        pos = ti - jnp.where(si == 0, 0, jnp.where(si == 1, l0, l0 + l1))
        lane = jnp.bitwise_and(tj, 31).astype(F32)
        ang = pos.astype(F32) * jnp.exp(lane * (-math.log(10000.0) / 32))
        co, si_ = jnp.cos(ang), jnp.sin(ang)
        si_ = jnp.where(jnp.bitwise_and(tj, 63) < 32, -si_, si_)
        s.cos[...] = jnp.concatenate([co] * 4, axis=1)
        s.sin[...] = jnp.concatenate([si_] * 4, axis=1)
        x = s.hid[...]
        nrm = (x * rinv(x) * s.gp[0:1]).astype(BF)
        s.nrm[...] = nrm

    def swap(s, v):
        lane = jnp.bitwise_and(iota((128, 512), 1), 63)
        return jnp.where(lane < 32, pltpu.roll(v, 512 - 32, 1), pltpu.roll(v, 32, 1))

    def attention(s):
        nrm = s.nrm[...]
        rs = rsum(nrm)
        allow = jnp.concatenate([s.allow[...]] * 7, axis=0)
        for b in range(3):
            w = units(s.codes(0, 5), b)
            lin = (nn(nrm, w) * MUL[b] + OFF[b] * rs) * s.qkv_scale[...]
            s.lin[b] = lin
            qk = lin[:, :512]
            qk = (qk * s.cos[...] + s.swap(qk) * s.sin[...]).astype(BF)
            qs = jnp.concatenate([qk[:, 64 * i:64 * i + 64] for i in range(7)], axis=0)
            k = qk[:, 448:512]
            v = lin[:, 512:576].astype(BF)
            s.qs[b], s.k[b], s.v[b] = qs, k, v
            th = jnp.tanh(nt(qs, k) * (0.125 / CAP))
            e = jnp.exp(CAP * th) * allow
            pr = e / jnp.sum(e, axis=-1, keepdims=True)
            s.th[b], s.pr[b] = th, pr
            mx = nn(pr.astype(BF), v).astype(BF)
            mixed = jnp.concatenate([jnp.zeros((128, 64), BF)] + [mx[128 * i:128 * i + 128] for i in range(7)], axis=1)
            s.mixed[pl.ds(128 * b, 128)] = mixed
            wo = units(s.codes(4, 4), b)
            s.acc[pl.ds(128 * b, 128)] = nt(mixed, wo) * MUL[b] + OFF[b] * rsum(mixed)

    def middle(s):
        s.bu[...] = s.exchange(0, s.acc[...])
        for b in range(3):
            d = pl.ds(128 * b, 128)
            br = s.bu[d] * s.so[...]
            lif = s.hid[...] + br * rinv(br) * s.gp[1:2]
            s.lifted[d] = lif
            n2 = (lif * rinv(lif) * s.gp[2:3]).astype(BF)
            s.n2[d] = n2
            s.rsn[d] = jnp.broadcast_to(rsum(n2), (128, 128))
        s.n2t[...] = s.n2[...].T
        s.acc[...] = jnp.zeros_like(s.acc)
        s.asum[...] = jnp.zeros_like(s.asum)

    def srow(s, ref, k, n): return ref[:, pl.ds(pl.multiple_of(k * 128, 128), n * 128)]

    def ffn_fwd(s, k, n):
        wg, wu, wd = s.codes(GATE + k, n), s.codes(UP + k, n), s.codes(DOWN + k, n)
        sg, su = s.srow(s.g_scale, k, n), s.srow(s.u_scale, k, n)
        for b in range(3):
            d = pl.ds(128 * b, 128)
            n2, rs = s.n2[d], s.rsn[d][:, 0:1] * OFF[b]
            g = (nn(n2, units(wg, b)) * MUL[b] + rs) * sg
            u = (nn(n2, units(wu, b)) * MUL[b] + rs) * su
            act = (0.5 * g * (1.0 + jnp.tanh(C0 * (g + C1 * g * g * g))) * u).astype(BF)
            for i in range(n):
                c = slice(128 * i, 128 * i + 128)
                s.g[k + i, d], s.u[k + i, d], s.act[k + i, d] = g[:, c].astype(s.g.dtype), u[:, c].astype(s.g.dtype), act[:, c]
            s.acc[d] += nt(act, units(wd, b)) * MUL[b]
            s.asum[d] += jnp.broadcast_to(rsum(act) * OFF[b], (128, 128))

    def turn(s):
        fu = s.exchange(1, s.acc[...] + s.asum[...][:, 0:1])
        dgain, dsd = 0.0, 0.0
        for b in range(3):
            d = pl.ds(128 * b, 128)
            f = fu[128 * b:128 * b + 128]
            feed = f * s.sd[...]
            r = rinv(feed)
            lif = s.lifted[d]
            res = (lif + feed * r * s.gp[3:4]).astype(BF)
            s.result[b] = nt(res, s.p[...]).astype(BF)
            dy = nn(s.cot[b], s.p[...])
            s.dy[d] = dy.astype(BF)
            df, dg = rms_back(feed, r, s.gp[3:4], dy)
            dgain += dg
            dfl = df.astype(BF)
            dsd += csum(dfl.astype(F32) * f)
            s.dfl[d] = dfl
            dfs = (df * s.sd[...]).astype(BF)
            s.dfs[d] = dfs
            s.rsn[d] = jnp.broadcast_to(rsum(dfs) * OFF[b], (128, 128))
        s.sm[11:12] = dgain
        s.sm[7:8] = dsd
        s.dft[...] = s.dfl[...].T
        s.acc[...] = jnp.zeros_like(s.acc)
        s.asum[...] = jnp.zeros_like(s.asum)

    def ffn_bwd(s, k, n):
        wg, wu, wd = s.codes(GATE + k, n), s.codes(UP + k, n), s.codes(DOWN + k, n)
        sg, su = s.srow(s.g_scale, k, n), s.srow(s.u_scale, k, n)
        gl, ul, al = [], [], []
        gsum, usum = 0.0, 0.0
        get = lambda ref, d: jnp.concatenate([ref[k + i, d] for i in range(n)], axis=1)
        for b in range(3):
            d = pl.ds(128 * b, 128)
            da = nn(s.dfs[d], units(wd, b)) * MUL[b] + s.rsn[d][:, 0:1]
            g, u = get(s.g, d).astype(F32), get(s.u, d).astype(F32)
            t = jnp.tanh(C0 * (g + C1 * g * g * g))
            hp = 0.5 * (1.0 + t)
            du = da * (g * hp)
            dg = da * u * (hp + 0.5 * g * (1.0 - t * t) * C0 * (1.0 + 3 * C1 * g * g))
            dgl, dul = dg.astype(BF), du.astype(BF)
            gl.append(dgl); ul.append(dul); al.append(get(s.act, d))
            gsum += csum(dgl.astype(F32) * g); usum += csum(dul.astype(F32) * u)
            dgs, dus = (dg * sg).astype(BF), (du * su).astype(BF)
            s.acc[d] += (nt(dgs, units(wg, b)) + nt(dus, units(wu, b))) * MUL[b]
            s.asum[d] += jnp.broadcast_to((rsum(dgs) + rsum(dus)) * OFF[b], (128, 128))
        at = lambda ref: ref.at[:, pl.ds(pl.multiple_of(k * 128, 128), n * 128)]
        at(s.gsg)[...] = gsum / sg
        at(s.usg)[...] = usum / su
        gl, ul, al = (jnp.concatenate(t, axis=0) for t in (gl, ul, al))
        for base, lhs, rhs in ((GATE, s.n2t, gl), (UP, s.n2t, ul), (DOWN, s.dft, al)):
            dw = nn(lhs[...], rhs).astype(BF)
            for i in range(n):
                s.dw[base + k + i] = dw[:, 128 * i:128 * i + 128].reshape(s.dw.shape[1:])

    def lower(s):
        valid = jnp.where(jnp.bitwise_and(iota((1, 1024), 1), 15) < 14, 1.0, 0.0)
        dn = s.exchange(2, (s.acc[...] + s.asum[...][:, 0:1]) * valid)
        dg1, dg2, dso, din = 0.0, 0.0, 0.0, 0.0
        for b in range(3):
            d = pl.ds(128 * b, 128)
            lif = s.lifted[d]
            dl, dg = rms_back(lif, rinv(lif), s.gp[2:3], dn[128 * b:128 * b + 128])
            dg2 += dg
            dl = dl + s.dy[d].astype(F32)
            din = din + dl
            bu = s.bu[d]
            br = bu * s.so[...]
            db, dg = rms_back(br, rinv(br), s.gp[1:2], dl)
            dg1 += dg
            dbl = db.astype(BF)
            dso += csum(dbl.astype(F32) * bu)
            s.dbl[d] = dbl
            s.dbs[d] = (db * s.so[...]).astype(BF)
        s.din[...] = din
        s.sm[9:10], s.sm[10:11], s.sm[6:7] = dg1, dg2, dso

    def attention_back(s):
        nsum, dqk, dv, sg = 0.0, 0.0, 0.0, 0.0
        dn = 0.0
        scale = s.qkv_scale[...]
        for b in range(3):
            d = pl.ds(128 * b, 128)
            dbs = s.dbs[d]
            dm = (nn(dbs, units(s.codes(4, 4), b)) * MUL[b] + OFF[b] * rsum(dbs)).astype(BF)
            dms = jnp.concatenate([dm[:, 64 * i + 64:64 * i + 128] for i in range(7)], axis=0)
            th, pr = s.th[b], s.pr[b]
            k, v, qs = s.k[b], s.v[b], s.qs[b]
            dp = nt(dms, v)
            gv = tn(pr.astype(BF), dms)
            dc = pr * (dp - jnp.sum(dp * pr, axis=-1, keepdims=True))
            dr = (dc * (1.0 - th * th)).astype(BF)
            gq = nn(dr, k) * 0.125
            gk = tn(dr, qs) * 0.125
            gqk = jnp.concatenate([gq[128 * i:128 * i + 128] for i in range(7)] + [gk], axis=1)
            gqk = gqk * s.cos[...] - s.swap(gqk) * s.sin[...]
            g = jnp.concatenate([gqk, gv, jnp.zeros((128, 64), F32)], axis=1)
            gl = g.astype(BF)
            gs = (g * scale).astype(BF)
            dn += nt(gs, units(s.codes(0, 5), b)) * MUL[b]
            nsum += rsum(gs) * OFF[b]
            sg += csum(gl.astype(F32) * s.lin[b])
            dqk += gl.astype(F32)
        s.sm[12:13, 0:640] = jnp.where(scale > 0, sg / scale, 0.0)
        valid = jnp.where(jnp.bitwise_and(iota((1, 1024), 1), 15) < 14, 1.0, 0.0)
        nrmt = s.nrm[...].T
        dqk = dqk.astype(BF)
        dw = nn(nrmt, dqk[:, :512]).astype(BF)
        lhs = jnp.concatenate([nrmt, s.dbl[...].T], axis=1)
        rhs = jnp.concatenate([jnp.concatenate([dqk[:, 512:576], jnp.zeros((128, 448), BF)], axis=1), s.mixed[...]], axis=0)
        dw2 = nn(lhs, rhs).astype(BF)
        part = (dn + nsum) * valid
        for i in range(4):
            s.dw[i] = dw[:, 128 * i:128 * i + 128].reshape(s.dw.shape[1:])
            s.dw[4 + i] = dw2[:, 128 * i:128 * i + 128].reshape(s.dw.shape[1:])
        d1 = s.exchange(3, part)
        x = s.hid[...]
        dx, dg = rms_back(x, rinv(x), s.gp[0:1], d1)
        s.sm[8:9] = dg
        s.in_grad[...] = nt((s.din[...] + dx).astype(BF), s.p[...]).astype(BF)

INS = ("hidden", "cot", "lengths", "gains", "qkv_scale", "o_scale", "g_scale", "u_scale", "d_scale")
def comp_scratch(gdt=F32):
    V = pltpu.VMEM
    return dict(
        p=V((896, 1024), BF), gp=V((4, 1024), F32), so=V((1, 1024), F32), sd=V((1, 1024), F32), hid=V((128, 1024), F32),
        allow=V((128, 128), F32), cos=V((128, 512), F32), sin=V((128, 512), F32), nrm=V((128, 1024), BF),
        lin=V((3, 128, 640), F32), qs=V((3, 896, 64), BF), k=V((3, 128, 64), BF), v=V((3, 128, 64), BF),
        th=V((3, 896, 128), F32), pr=V((3, 896, 128), F32), mixed=V((384, 512), BF), acc=V((384, 1024), F32),
        bu=V((384, 1024), F32), lifted=V((384, 1024), F32), n2=V((384, 1024), BF), rsn=V((384, 128), F32), n2t=V((1024, 384), BF),
        asum=V((384, 128), F32), g=V((19, 384, 128), gdt), u=V((19, 384, 128), gdt), act=V((19, 384, 128), BF),
        dy=V((384, 1024), BF), dfl=V((384, 1024), BF), dfs=V((384, 1024), BF), dft=V((1024, 384), BF),
        gsg=V((1, 2432), F32), usg=V((1, 2432), F32), dbl=V((384, 1024), BF), dbs=V((384, 1024), BF), din=V((128, 1024), F32),
        xs=V((4, 384, 1024), BF), xr=V((4, 384, 1024), BF),
        xss=pltpu.SemaphoreType.DMA((4,)), xrs=pltpu.SemaphoreType.DMA((4,)))

def comp_body(names, *refs):
    r = dict(zip(names, refs))
    s = Comp(h=Here(), **r)
    b = pltpu.get_barrier_semaphore()
    pl.semaphore_signal(b, inc=1, device_id=(s.h.dp, 1 - s.h.mp), device_id_type=MESH)
    pl.semaphore_wait(b, 1)
    cp = pltpu.make_async_copy(s.w_in, s.w, s.lsem.at[0]); cp.start()
    s.dw = s.w
    s.sm[...] = jnp.zeros_like(s.sm)
    s.prologue()
    cp.wait()
    s.attention(); s.middle()
    @pl.loop(0, 9)
    def _(j): s.ffn_fwd(2 * j, 2)
    s.ffn_fwd(18, 1)
    s.turn()
    @pl.loop(0, 9)
    def _(j): s.ffn_bwd(2 * j, 2)
    s.ffn_bwd(18, 1)
    s.pack()
    s.lower(); s.attention_back()
    cp = pltpu.make_async_copy(s.w, s.dw_out, s.lsem.at[1]); cp.start(); cp.wait()

def pack(s):
    for i in range(3):
        m = min(1024, 2432 - 1024 * i)
        s.sm[i:i + 1, 0:m] = s.gsg[:, 1024 * i:1024 * i + m]
        s.sm[3 + i:4 + i, 0:m] = s.usg[:, 1024 * i:1024 * i + m]
Comp.pack = pack

def compute(w, ins, cid=2):
    V = pl.BlockSpec(memory_space=pltpu.VMEM)
    A = pl.BlockSpec(memory_space=pl.ANY)
    sc = dict(comp_scratch(), w=pltpu.VMEM((65, 4, 4, 4, 16, 128), BF), lsem=pltpu.SemaphoreType.DMA((2,)))
    names = ("w_in",) + INS + ("dw_out", "result", "in_grad", "sm") + tuple(sc)
    return pl.pallas_call(
        functools.partial(comp_body, names),
        out_shape=(jax.ShapeDtypeStruct((65, 4, 4, 4, 16, 128), BF), jax.ShapeDtypeStruct((3, 128, 896), BF),
                   jax.ShapeDtypeStruct((128, 896), BF), jax.ShapeDtypeStruct((16, 1024), F32)),
        in_specs=[A] + [pl.BlockSpec(memory_space=pltpu.SMEM) if n == "lengths" else V for n in INS],
        out_specs=(A, V, V, V),
        scratch_shapes=list(sc.values()),
        compiler_params=pltpu.CompilerParams(collective_id=cid, has_side_effects=True, vmem_limit_bytes=63 << 20),
    )(w, *ins)
GROUPS = ((0, 22), (22, 22), (44, 21))
CHUNKS = (((0, 22),), ((0, 22),), ((0, 21),))

def local(hidden_in, cotangent, lengths, gains, query_codes, key_codes, value_codes, output_codes, gate_codes, upward_codes, down_codes,
          query_scale, key_scale, value_scale, output_scale, gate_scale, upward_scale, down_scale):
    block = jnp.concatenate([query_codes, key_codes, value_codes, output_codes.T, gate_codes, upward_codes, down_codes.T], axis=1)
    block = jnp.pad(block, ((0, 2), (0, 0))).reshape(16, 65, 128).transpose(1, 0, 2)
    w = gather(block, GROUPS, CHUNKS)
    row = lambda *a: jnp.concatenate(a)[None]
    ins = (hidden_in, cotangent, lengths, gains, row(query_scale, key_scale, value_scale, jnp.zeros((64,), F32)), output_scale[None],
           gate_scale[None], upward_scale[None], down_scale[None])
    dw, result, in_grad, sm = compute(w, ins)
    grads, sm = scatter(dw, sm, GROUPS, CHUNKS)
    g = grads.transpose(1, 0, 2).reshape(16, 65 * 128)[:14]
    p = spread_matrix()
    back = nt_hi(sm, p)
    flat = lambda r: sm[r:r + 3].reshape(3072)[:2432]
    return (result, in_grad, g[:, :448], g[:, 448:512], g[:, 512:576], g[:, 576:1024].T, g[:, 1024:3456], g[:, 3456:5888], g[:, 5888:].T,
            sm[12, :448], sm[12, 448:512], sm[12, 512:576], back[6], flat(0), flat(3), back[7], back[8:12])

def solution(mesh):
    d, c, r = P("dp", None), P("dp", "mp"), P("mp", "dp")
    return jax.shard_map(local, mesh=mesh,
        in_specs=(d, P(None, "dp", None), d, P(), c, c, c, r, c, c, r, P("mp"), P("mp"), P("mp"), P(), P("mp"), P("mp"), P()),
        out_specs=(P(None, "dp", None), d, c, c, c, r, c, c, r, P("mp"), P("mp"), P("mp"), P(), P("mp"), P("mp"), P(), P()),
        check_vma=False)
```

time: 2060 us -> 271 us (0.13)
  blocking collectives: 1340 us -> 0 us
  Pallas kernels: 0 us -> 254 us
  local copies, waits for them, and re-layouts: 214 us -> 12.5 us
  waiting for transfers between devices: 172 us -> 0 us
  matrix products: 173 us -> 4.26 us
  other arithmetic: 67.9 us -> 0.08 us
  starting transfers between devices: 58.5 us -> 0 us
    all_gather x4 -> x0, blocking collectives: 702 us -> none  [the longest x1 180 us: local(): lax.all_gather(value_codes, 'dp', axis=0, tiled=True)]
    psum x2 -> x0, blocking collectives: 345 us -> none  [the longest x1 342 us: local(): lax.psum((query_scale_grad, key_scale_grad, value_scale_grad, output_scal...]
    unnamed x1 -> x0, blocking collectives: 295 us -> none
    pallas_call x0 -> x3, Pallas kernels: none -> 254 us  [the longest x1 92.7 us: scatter(): pl.pallas_call(functools.partial(scatter_body, groups, chunks), out_shape...]
    dot_general x81 -> x1, matrix products: 173 us -> 4.26 us  [nt_hi(): lax.dot_general(a, b, (((1,), (1,)), ((), ())), preferred_element_type=F3...]
    all_gather x3 -> x0, waiting for transfers between devices: 142 us -> none  [the longest x1 49.1 us: local(): lax.all_gather(upward_codes, 'dp', axis=0, tiled=True)]
    sub x28 -> x0, local copies, waits for them, and re-layouts: 115 us -> none  [code_units(): jnp.floor(code_set.astype(jnp.float32) / bin_size) + 0.5]
    unnamed x17 -> x0, starting transfers between devices: 57.6 us -> none
  transfers between devices with their start and end apart: 24 -> 0, of which waited for: 6 -> 0; matrix products, arithmetic and copies ran while one was open for 23% -> 0% of each run, Pallas kernels for 0% -> 0%
where the time goes in v1:
time: 271 us
  Pallas kernels  254 us (94%)
  local copies, waits for them, and re-layouts  12.5 us (5%)
  matrix products  4.26 us (2%)
    pallas_call x1, Pallas kernels, scatter(): pl.pallas_call(functools.partial(scatter_body, groups, chunks), out_shape...  92.7 us
    pallas_call x1, Pallas kernels, gather(): pl.pallas_call(functools.partial(gather_body, nslab, groups, chunks3), ou...  83.9 us
    pallas_call x1, Pallas kernels, compute(): pl.pallas_call(functools.partial(comp_body, names), out_shape=(jax.ShapeD...  77 us

profile of v1, /device:TPU:0, one launch (start us, length us, event | category | flops | bytes accessed | tf_op | source)
XLA Modules:
  0.0 271.2 jit_solution(6520864625557919471)
XLA Ops:
  0.7 1.1 concatenate.6
  1.8 0.8 bitcast_bitcast_fusion.s_ref
  2.5 0.0 copy-start.4
  2.5 0.0 copy-start.5
  2.5 0.0 copy-start.8
  2.5 0.0 copy-start.9
  2.5 0.0 copy-start.10
  2.6 0.0 copy-start.6
  2.6 0.0 copy-start.7
  2.6 83.9 %shard_map.305.refs_0_ = bf16[65,4,4,4,16,128]{5,4,3,2,1,0:T(8,128)(2,1)} custom-call(bf16[65,16,128]{2,1,0:T(8,128)(2,1)} %bitcast_bitcast_fusion.s_ref), custom_call_target="tpu_custom_call" | custom-call | tf_op jit(solution)/shard_map/pallas_call | solution.py:87
  86.5 0.0 copy-done.4
  86.5 0.6 broadcast_in_dim.29.refs_7_
  87.1 0.0 copy-done.5
  87.1 0.6 broadcast_in_dim.30.refs_8_
  87.7 0.0 copy-done.8
  87.7 0.0 copy-done.9
  87.7 0.0 copy-done.10
  87.7 0.1 pad_maximum_fusion
  87.8 0.6 broadcast_in_dim.27.refs_5_
  88.4 0.0 copy-done.6
  88.4 0.6 broadcast_in_dim.28.refs_6_
  89.0 0.0 copy-done.7
  89.0 0.6 broadcast_in_dim.31.refs_9_
  89.5 77.0 %shard_map.306 = (bf16[65,4,4,4,16,128]{5,4,3,2,1,0:T(8,128)(2,1)}, bf16[3,128,896]{2,1,0:T(8,128)(2,1)}, bf16[128,896]{1,0:T(8,128)(2,1)}, f32[16,1024]{1,0:T(8,128)}) custom-call(bf16[65,4,4,4,16,128]{5,4,3,2,1,0:T(8,128)(2,1)} %shard_map.305.refs_0_, bf16[128,896]{1,0:T(8,128)(2,1)} %refs_1_.1, bf16[3,128,896]{2,1,0:T(8,128)(2,1)} %refs_2_.1, ...), custom_call_target="tpu_custom_call" | custom-call | tf_op jit(solution)/shard_map/pallas_call | solution.py:493
  166.5 92.7 %shard_map.307 = (f32[65,16,128]{2,1,0:T(8,128)}, f32[16,1024]{1,0:T(8,128)}) custom-call(bf16[65,4,4,4,16,128]{5,4,3,2,1,0:T(8,128)(2,1)} %get-tuple-element.25.g_ref, f32[16,1024]{1,0:T(8,128)} %get-tuple-element.26.sm_ref), custom_call_target="tpu_custom_call" | custom-call | tf_op jit(solution)/shard_map/pallas_call | solution.py:184
  259.2 0.0 copy-start.1
  259.2 0.0 copy-start.3
  259.2 0.0 copy-start
  259.3 4.3 %fusion = f32[16,896]{1,0:T(8,128)S(1)} fusion(f32[16,1024]{1,0:T(8,128)} %get-tuple-element.28, s32[896]{0:T(1024)S(1)} %shift-right-logical_multiply_fusion), kind=kOutput, calls=%fused_computation | convolution fusion | flops 178913280 | bytes 126464 | tf_op jit(solution)/shard_map/dot_general | solution.py:207
  263.5 0.0 copy-start.2
  263.5 0.6 slice_reduce_fusion
  264.1 0.0 copy-done.1
  264.2 0.2 copy.36
  264.4 0.1 copy.38
  264.5 0.8 slice_bitcast_fusion
  265.2 0.6 slice.88
  265.9 0.0 copy-done.3
  265.9 0.6 reshape.46
  266.5 0.6 reshape.47
  267.1 0.6 slice_bitcast_fusion.2
  267.7 0.7 slice_bitcast_fusion.1
  268.4 0.7 fusion.7
  269.0 0.6 slice.66
  269.6 0.0 copy-done
  269.6 0.8 copy.42
  270.5 0.0 copy-done.2
  270.5 0.7 copy.43
  (4 shorter events, 0.1 us)
Async XLA Ops:
  2.5 83.9 %copy-start.4 = (f32[2432]{0:T(1024)S(1)}, f32[2432]{0:T(1024)}, u32[]{:S(2)}) copy-start(f32[2432]{0:T(1024)} %param.33) | copy-start | bytes 29188
  2.5 84.5 %copy-start.5 = (f32[2432]{0:T(1024)S(1)}, f32[2432]{0:T(1024)}, u32[]{:S(2)}) copy-start(f32[2432]{0:T(1024)} %param.34) | copy-start | bytes 29188
  2.5 85.2 %copy-start.8 = (f32[448]{0:T(512)S(1)}, f32[448]{0:T(512)}, u32[]{:S(2)}) copy-start(f32[448]{0:T(512)} %param.29) | copy-start | bytes 5380
  2.5 85.2 %copy-start.9 = (f32[64]{0:T(128)S(1)}, f32[64]{0:T(128)}, u32[]{:S(2)}) copy-start(f32[64]{0:T(128)} %param.31) | copy-start | bytes 772
  2.5 85.2 %copy-start.10 = (f32[64]{0:T(128)S(1)}, f32[64]{0:T(128)}, u32[]{:S(2)}) copy-start(f32[64]{0:T(128)} %param.30) | copy-start | bytes 772
  2.6 85.8 %copy-start.6 = (f32[896]{0:T(1024)S(1)}, f32[896]{0:T(1024)}, u32[]{:S(2)}) copy-start(f32[896]{0:T(1024)} %param.32) | copy-start | bytes 10756
  2.6 86.4 %copy-start.7 = (f32[896]{0:T(1024)S(1)}, f32[896]{0:T(1024)}, u32[]{:S(2)}) copy-start(f32[896]{0:T(1024)} %param.35) | copy-start | bytes 10756
  259.2 4.9 %copy-start.1 = (f32[65,16,128]{2,1,0:T(8,128)S(1)}, f32[65,16,128]{2,1,0:T(8,128)}, u32[]{:S(2)}) copy-start(f32[65,16,128]{2,1,0:T(8,128)} %get-tuple-element.27) | copy-start | bytes 1597444
  259.2 6.6 %copy-start.3 = (f32[16,1024]{1,0:T(8,128)S(1)}, f32[16,1024]{1,0:T(8,128)}, u32[]{:S(2)}) copy-start(f32[16,1024]{1,0:T(8,128)} %get-tuple-element.28) | copy-start | bytes 196612
  259.2 10.4 %copy-start = (bf16[3,128,896]{2,1,0:T(8,128)(2,1)S(1)}, bf16[3,128,896]{2,1,0:T(8,128)(2,1)}, u32[]{:S(2)}) copy-start(bf16[3,128,896]{2,1,0:T(8,128)(2,1)} %get-tuple-element.59) | copy-start | bytes 2064388
  263.5 7.0 %copy-start.2 = (bf16[128,896]{1,0:T(8,128)(2,1)S(1)}, bf16[128,896]{1,0:T(8,128)(2,1)}, u32[]{:S(2)}) copy-start(bf16[128,896]{1,0:T(8,128)(2,1)} %get-tuple-element.60) | copy-start | bytes 688132
